TPU v7x, 32 devices: a whole 2x2x4 slice. The times are simulated.
32 devices in a mesh: groups: 2 (over y), rows: 4 (over z), cols: 2 (over x), sub: 2 (over core).
Axes of the slice: x: 2, y: 2, z: 4, core: 2. Of those that a mesh axis runs over, the one named last changes fastest.
Arguments:
- scf_blocks: bfloat16 [4096, 128, 128], P(('groups', 'rows', 'cols', 'sub')), parts along dimension 0, may hold values from -0.125 to 0.125
- scf_source: int32 [256, 16], P(('groups', 'rows', 'sub'), 'cols'), parts along dimension 0, may hold values from 0 to 127, as said below
- pattern: int32 [256, 16], P(('groups', 'rows', 'sub'), 'cols'), parts along dimension 0, may hold values from 0 to 127, as said below
- panel: bfloat16 [32768, 128], P(('groups', 'rows', 'sub')), parts along dimension 0, may hold values from -6 to 6
Outputs:
- cheb_one: bfloat16 [32768, 128], P(('groups', 'rows', 'sub')), parts along dimension 0
- cheb_two: bfloat16 [32768, 128], P(('groups', 'rows', 'sub')), parts along dimension 0
There are 2 independent parts, one for each index of `groups`. A program takes and returns all parts, laid end to end along the dimension named above; each array names one. Nothing has to cross between parts.
Inputs may be any that keep to these rules, and one draw needn't show every extreme that they name: `pattern`: the 16 block columns of each block row are distinct, each within 16 blocks of the row's own index counted cyclically over the 128 block rows, and every block row has one at offset 0, one at -16 and one at +16. `scf_source`: each device's tile of 16 x 8 entries is a permutation of 0 to 127.
All inputs are finite; a program needn't handle non-finite values.
Results may differ from a plain program's by a relative error of at most 0.0046.
Values may be sent and summed in bfloat16 or wider, within the bound.
A program may use at most 64 MiB of HBM per device.

v0:
```python
import jax
import jax.numpy as jnp
from jax import lax
from jax.sharding import PartitionSpec as P


def padded(cells, sides, width):
    for axis, dim in sides:
        count = lax.axis_size(axis)
        head = lax.slice_in_dim(cells, 0, width, axis=dim)
        tail = lax.slice_in_dim(cells, cells.shape[dim] - width, cells.shape[dim], axis=dim)
        cells = jnp.concatenate(
            [
                lax.ppermute(tail, axis, [(i, (i + 1) % count) for i in range(count)]),
                cells,
                lax.ppermute(head, axis, [((i + 1) % count, i) for i in range(count)]),
            ],
            axis=dim,
        )
    return cells


def local(scf_blocks, scf_source, pattern, panel):
    br_dev, kb_col = pattern.shape
    block_len = scf_blocks.shape[1]
    width = panel.shape[1]
    slot_order = scf_source.reshape(-1)
    count_rows = lax.axis_size("rows")
    count_sub = lax.axis_size("sub")
    received = lax.all_to_all(scf_blocks, ("rows", "sub"), split_axis=0, concat_axis=0, tiled=True)
    blocks = jnp.take(received, slot_order, axis=0)
    blocks = blocks.reshape(br_dev, kb_col, block_len, block_len)
    total_tiles = br_dev * count_rows * count_sub
    owner_index = lax.axis_index("rows") * count_sub + lax.axis_index("sub")
    first_tile = owner_index * br_dev
    local_cols = (pattern - first_tile + br_dev + total_tiles) % total_tiles
    local_cols = local_cols.reshape(-1)

    def multiply(operand):
        extended = padded(operand, ((("rows", "sub"), 0),), br_dev * block_len)
        tile_stack = extended.reshape(3 * br_dev, block_len, width)
        picked = jnp.take(tile_stack, local_cols, axis=0).reshape(br_dev, kb_col, block_len, width)
        products = jnp.einsum("bkij,bkjc->bic", blocks, picked, preferred_element_type=jnp.float32)
        return products.reshape(br_dev * block_len, width)

    def combine_cols(partial_value, factor, subtract):
        summed = lax.psum(partial_value, "cols")
        return (factor * summed - subtract.astype(jnp.float32)).astype(jnp.bfloat16)

    cheb_one = combine_cols(multiply(panel), 1.0, jnp.zeros_like(panel))
    cheb_two = combine_cols(multiply(cheb_one), 2.0, panel)
    return (cheb_one, cheb_two)


def solution(mesh):
    return jax.shard_map(
        local,
        mesh=mesh,
        in_specs=(
            P(("groups", "rows", "cols", "sub"), None, None),
            P(("groups", "rows", "sub"), "cols"),
            P(("groups", "rows", "sub"), "cols"),
            P(("groups", "rows", "sub"), None),
        ),
        out_specs=(P(("groups", "rows", "sub"), None), P(("groups", "rows", "sub"), None)),
        check_vma=False,
    )
```

profile of v0, /device:TPU:11, one launch (start us, length us, event | category | flops | bytes accessed | tf_op | source)
XLA Modules:
  0.0 222.8 jit_solution(5499753586347357151)
XLA Ops:
  7.2 0.0 copy-start.2
  7.2 0.0 copy-start.3
  7.2 0.0 copy-start.4
  7.2 5.8 %all-to-all-start = ((bf16[128,128,128]{2,1,0:T(8,128)(2,1)}), bf16[128,128,128]{2,1,0:T(8,128)(2,1)}, u32[]{:S(2)}, u32[]{:S(2)}) async-start(bf16[128,128,128]{2,1,0:T(8,128)(2,1)} %param.6), calls=%async_computation | async-start | bytes 8388608 | tf_op jit(solution)/shard_map/all_to_all | solution.py:30
  13.0 0.0 all-reduce.3.cloned.1.call-start
  13.0 0.0 copy-done.2
  13.0 0.4 collective-permute-start.1
  13.4 1.4 collective-permute-start
  14.8 0.0 copy-done.3
  14.8 0.1 copy.10
  14.9 0.1 copy.9
  15.0 0.0 copy-done.4
  15.0 0.1 copy.11
  15.0 0.1 reshape.72
  15.1 0.1 reshape.70
  15.3 101.1 %collective-permute-done.1 = bf16[2048,128]{1,0:T(8,128)(2,1)S(1)} collective-permute-done((bf16[2048,128]{1,0:T(8,128)(2,1)S(1)}, bf16[2048,128]{1,0:T(8,128)(2,1)S(1)}, u32[]{:S(2)}, u32[]{:S(2)}) %collective-permute-start.1) | collective-permute-done | bytes 524320 | tf_op jit(solution)/shard_map/ppermute | solution.py:16
  116.4 0.0 collective-permute-done
  116.4 0.1 pad_maximum_fusion
  116.5 3.0 %gather_fusion.1 = bf16[128,128,128]{2,1,0:T(8,128)(2,1)} fusion(bf16[48,128,128]{2,1,0:T(8,128)(2,1)S(1)} %bitcast.18, s32[1024]{0:T(1024)S(1)} %pad_clamp_fusion), kind=kCustom, calls=%fused_computation.clone | custom fusion | bytes 8389120 | tf_op jit(solution)/shard_map/jit(_take)/gather | solution.py:42
  119.6 4.6 %broadcast_select_fusion.1 = bf16[128,128,128]{2,1,0:T(8,128)(2,1)} fusion(bf16[128,128,128]{2,1,0:T(8,128)(2,1)} %gather_fusion.1, pred[128]{0:T(512)(128)(4,1)S(1)} %compare_and_fusion.1), kind=kLoop, calls=%fused_computation.4 | loop fusion | flops 2097152 | bytes 8388736 | tf_op jit(solution)/shard_map/jit(_take)/select_n | solution.py:42
  124.2 0.0 all-to-all-done
  124.2 5.3 %gather_fusion = bf16[128,128,128]{2,1,0:T(8,128)(2,1)} fusion(bf16[128,128,128]{2,1,0:T(8,128)(2,1)} %all-to-all-done, s32[1024]{0:T(1024)S(1)} %pad_clamp_fusion.1), kind=kCustom, calls=%fused_computation.2 | custom fusion | bytes 8389120 | tf_op jit(solution)/shard_map/jit(_take)/gather | solution.py:31
  129.4 4.8 %fusion.1 = f32[16,128,128,1]{2,1,3,0:T(8,128)S(1)} fusion(bf16[16,8,128,128]{3,2,1,0:T(8,128)(2,1)} %bitcast.21, bf16[16,8,128,128]{3,2,1,0:T(8,128)(2,1)} %bitcast.19, pred[16,8]{1,0:T(8,128)(4,1)S(1)} %copy.9), kind=kOutput, calls=%fused_computation.7 | convolution fusion | flops 538968064 | bytes 9437312 | tf_op jit(solution)/shard_map/bkij,bkjc->bic/dot_general | solution.py:43
  134.2 17.8 %all-reduce.4 = bf16[2048,128]{1,0:T(8,128)(2,1)S(1)} all-reduce(f32[2048,128]{1,0:T(8,128)S(1)} %bitcast.23), channel_id=1, replica_groups=mesh['groups'=2,'rows'=4,'cols'=2,'sub'=2] {'cols'}, use_global_device_ids=true, to_apply=%region_0.0 | all-reduce | flops 262144 | bytes 1572864 | tf_op jit(solution)/shard_map/psum | solution.py:47
  152.0 0.0 copy-start.1
  152.0 0.1 collective-permute-start.3
  152.1 2.6 %collective-permute-start.2 = (bf16[2048,128]{1,0:T(8,128)(2,1)S(1)}, bf16[2048,128]{1,0:T(8,128)(2,1)S(1)}, u32[]{:S(2)}, u32[]{:S(2)}) collective-permute-start(bf16[2048,128]{1,0:T(8,128)(2,1)S(1)} %all-reduce.4), channel_id=1, source_target_pairs={{0,1},{1,4},{4,5},{5,8},{8,9},{9,12},{12,13},{13,0},{2,3},{3,6},{6... | collective-permute-start | bytes 1572872 | tf_op jit(solution)/shard_map/ppermute | solution.py:14
  154.7 11.4 %collective-permute-done.3 = bf16[2048,128]{1,0:T(8,128)(2,1)S(1)} collective-permute-done((bf16[2048,128]{1,0:T(8,128)(2,1)S(1)}, bf16[2048,128]{1,0:T(8,128)(2,1)S(1)}, u32[]{:S(2)}, u32[]{:S(2)}) %collective-permute-start.3) | collective-permute-done | bytes 524320 | tf_op jit(solution)/shard_map/ppermute | solution.py:16
  166.1 0.0 collective-permute-done.2
  166.1 0.1 pad_maximum_fusion.1
  166.2 3.0 %gather_fusion.2 = bf16[128,128,128]{2,1,0:T(8,128)(2,1)} fusion(bf16[48,128,128]{2,1,0:T(8,128)(2,1)S(1)} %bitcast.17, s32[1024]{0:T(1024)S(1)} %pad_clamp_fusion), kind=kCustom, calls=%fused_computation.1.clone | custom fusion | bytes 8389120 | tf_op jit(solution)/shard_map/jit(_take)/gather | solution.py:42
  169.2 0.0 copy-done.1
  169.2 0.0 copy-start
  169.2 2.8 %broadcast_select_fusion = bf16[128,128,128]{2,1,0:T(8,128)(2,1)S(1)} fusion(bf16[128,128,128]{2,1,0:T(8,128)(2,1)} %gather_fusion.2, pred[128]{0:T(512)(128)(4,1)S(1)} %compare_and_fusion.1), kind=kLoop, calls=%fused_computation.3 | loop fusion | flops 2097152 | bytes 8388736 | tf_op jit(solution)/shard_map/jit(_take)/select_n | solution.py:42
  172.0 0.7 copy-done
  172.7 2.3 %fusion = f32[16,128,128,1]{2,1,3,0:T(8,128)} fusion(bf16[16,8,128,128]{3,2,1,0:T(8,128)(2,1)S(1)} %bitcast.22, bf16[16,8,128,128]{3,2,1,0:T(8,128)(2,1)S(1)} %bitcast.20, pred[16,8]{1,0:T(8,128)(4,1)S(1)} %copy.9), kind=kOutput, calls=%fused_computation.6 | convolution fusion | flops 538968064 | bytes 9437312 | tf_op jit(solution)/shard_map/bkij,bkjc->bic/dot_general | solution.py:43
  175.0 0.0 all-reduce.3.cloned.1.call-update
  175.0 38.7 %all-reduce.3.cloned.1.call-done = f32[2048,128]{1,0:T(8,128)} async-done(((f32[2048,128]{1,0:T(8,128)}), f32[2048,128]{1,0:T(8,128)}) %all-reduce.3.cloned.1.call-update) | async-done | bytes 1048592 | tf_op jit(solution)/shard_map/psum | solution.py:47
  213.8 2.2 subtract_convert_fusion
  (7 shorter events, 0.0 us)
Async XLA Ops:
  7.2 5.8 %copy-start.2 = (bf16[2048,128]{1,0:T(8,128)(2,1)S(1)}, bf16[2048,128]{1,0:T(8,128)(2,1)}, u32[]{:S(2)}) copy-start(bf16[2048,128]{1,0:T(8,128)(2,1)} %param.9) | copy-start | bytes 1572868
  7.2 7.6 %copy-start.3 = (s32[16,8]{0,1:T(8,128)S(1)}, s32[16,8]{0,1:T(8,128)}, u32[]{:S(2)}) copy-start(s32[16,8]{0,1:T(8,128)} %param.7) | copy-start | bytes 1540
  7.2 7.8 %copy-start.4 = (s32[16,8]{0,1:T(8,128)S(1)}, s32[16,8]{0,1:T(8,128)}, u32[]{:S(2)}) copy-start(s32[16,8]{0,1:T(8,128)} %param.8) | copy-start | bytes 1540
  7.2 117.0 %all-to-all-start = ((bf16[128,128,128]{2,1,0:T(8,128)(2,1)}), bf16[128,128,128]{2,1,0:T(8,128)(2,1)}, u32[]{:S(2)}, u32[]{:S(2)}) async-start(bf16[128,128,128]{2,1,0:T(8,128)(2,1)} %param.6), calls=%async_computation | async-start | bytes 8388608 | tf_op jit(solution)/shard_map/all_to_all | solution.py:30
  13.0 200.8 %all-reduce.3.cloned.1.call-start = ((), (), s32[]{:S(2)}) async-start(), calls=%async_computation.1 | async-start | bytes 2097152 | tf_op jit(solution)/shard_map/psum | solution.py:47
  13.0 103.5 %collective-permute-start.1 = (bf16[2048,128]{1,0:T(8,128)(2,1)S(1)}, bf16[2048,128]{1,0:T(8,128)(2,1)S(1)}, u32[]{:S(2)}, u32[]{:S(2)}) collective-permute-start(bf16[2048,128]{1,0:T(8,128)(2,1)S(1)} %copy-done.2), channel_id=1, source_target_pairs={{1,0},{4,1},{5,4},{8,5},{9,8},{12,9},{13,12},{0,13},{3,2},{6,3},{7... | collective-permute-start | bytes 1572872 | tf_op jit(solution)/shard_map/ppermute | solution.py:16
  13.4 103.0 %collective-permute-start = (bf16[2048,128]{1,0:T(8,128)(2,1)S(1)}, bf16[2048,128]{1,0:T(8,128)(2,1)S(1)}, u32[]{:S(2)}, u32[]{:S(2)}) collective-permute-start(bf16[2048,128]{1,0:T(8,128)(2,1)S(1)} %copy-done.2), channel_id=1, source_target_pairs={{0,1},{1,4},{4,5},{5,8},{8,9},{9,12},{12,13},{13,0},{2,3},{3,6},{6... | collective-permute-start | bytes 1572872 | tf_op jit(solution)/shard_map/ppermute | solution.py:14
  152.0 17.2 %copy-start.1 = (bf16[2048,128]{1,0:T(8,128)(2,1)}, bf16[2048,128]{1,0:T(8,128)(2,1)S(1)}, u32[]{:S(2)}) copy-start(bf16[2048,128]{1,0:T(8,128)(2,1)S(1)} %all-reduce.4) | copy-start | bytes 1572868
  152.0 14.0 %collective-permute-start.3 = (bf16[2048,128]{1,0:T(8,128)(2,1)S(1)}, bf16[2048,128]{1,0:T(8,128)(2,1)S(1)}, u32[]{:S(2)}, u32[]{:S(2)}) collective-permute-start(bf16[2048,128]{1,0:T(8,128)(2,1)S(1)} %all-reduce.4), channel_id=1, source_target_pairs={{1,0},{4,1},{5,4},{8,5},{9,8},{12,9},{13,12},{0,13},{3,2},{6,3},{7... | collective-permute-start | bytes 1572872 | tf_op jit(solution)/shard_map/ppermute | solution.py:16
  152.1 14.0 %collective-permute-start.2 = (bf16[2048,128]{1,0:T(8,128)(2,1)S(1)}, bf16[2048,128]{1,0:T(8,128)(2,1)S(1)}, u32[]{:S(2)}, u32[]{:S(2)}) collective-permute-start(bf16[2048,128]{1,0:T(8,128)(2,1)S(1)} %all-reduce.4), channel_id=1, source_target_pairs={{0,1},{1,4},{4,5},{5,8},{8,9},{9,12},{12,13},{13,0},{2,3},{3,6},{6... | collective-permute-start | bytes 1572872 | tf_op jit(solution)/shard_map/ppermute | solution.py:14
  169.2 3.4 %copy-start = (bf16[128,128,128]{2,1,0:T(8,128)(2,1)S(1)}, bf16[128,128,128]{2,1,0:T(8,128)(2,1)}, u32[]{:S(2)}) copy-start(bf16[128,128,128]{2,1,0:T(8,128)(2,1)} %gather_fusion) | copy-start | bytes 12582916
Sparse Core Ops, SparseCore 0:
  175.2 38.5 all-reduce.2
where the time goes:
time: 226 us; the launch traced here: 223 us
  waiting for transfers between devices  151 us (67%)
  blocking collectives  17.8 us (8%)
  between operations  14.1 us (6%)
  local copies, waits for them, and re-layouts  12.4 us (5%)
  starting transfers between devices  10.3 us (5%)
  other arithmetic  9.78 us (4%)
  matrix products  7.1 us (3%)
    ppermute x2, waiting for transfers between devices, padded(): lax.ppermute(head, axis, [((i + 1) % count, i) for i in range(count)])  113 us
    psum x1, waiting for transfers between devices, combine_cols(): summed = lax.psum(partial_value, 'cols')  38.7 us
    psum x1, blocking collectives, combine_cols(): summed = lax.psum(partial_value, 'cols')  17.8 us
    select_n x3, other arithmetic, multiply(): jnp.take(tile_stack, local_cols, axis=0)  7.38 us
    dot_general x2, matrix products, multiply(): jnp.einsum('bkij,bkjc->bic', blocks, picked, preferred_element_type=jnp.f...  7.1 us
    gather x2, local copies, waits for them, and re-layouts, multiply(): jnp.take(tile_stack, local_cols, axis=0)  6.06 us
    all_to_all x1, starting transfers between devices, local(): lax.all_to_all(scf_blocks, ('rows', 'sub'), split_axis=0, concat_axis=0,...  5.78 us
    gather x1, local copies, waits for them, and re-layouts, local(): blocks = jnp.take(received, slot_order, axis=0)  5.25 us
  transfers between devices with their start and end apart: 6, of which 3 were waited for; matrix products, arithmetic and copies ran while one was open for 4% of the time, Pallas kernels for 0%

commit v1 on v0

v1 whole, which is shorter than its diff:
```python
import jax
import jax.numpy as jnp
from jax import lax
from jax.experimental import pallas as pl
from jax.experimental.pallas import tpu as pltpu
from jax.sharding import PartitionSpec as P

MESH = pl.DeviceIdType.MESH


def kernel(
    blocks_ref, panel_ref, order_ref, cols_ref, one_ref, two_ref,
    recv, ext_one, ext_two, parts_one, parts_two,
    own_sem, block_send, block_recv, halo_send, halo_recv,
    next_send, next_recv, one_send, one_recv, two_send, two_recv,
):
    slots = blocks_ref.shape[0]
    br_dev = panel_ref.shape[0]
    kb_col = cols_ref.shape[0] // br_dev
    count_rows = lax.axis_size("rows")
    count_sub = lax.axis_size("sub")
    count_cols = lax.axis_size("cols")
    owners = count_rows * count_sub
    per_pair = slots // owners
    me = lax.axis_index("rows") * count_sub + lax.axis_index("sub")
    my_col = lax.axis_index("cols")

    def owner_id(owner):
        return {"rows": owner // count_sub, "sub": owner % count_sub}

    def col_id(hop):
        return {"cols": (my_col + hop) % count_cols}

    barrier = pltpu.get_barrier_semaphore()

    @pl.loop(1, owners)
    def _(hop):
        pl.semaphore_signal(barrier, inc=1, device_id=owner_id((me + hop) % owners), device_id_type=MESH)

    @pl.loop(1, count_cols)
    def _(hop):
        pl.semaphore_signal(barrier, inc=1, device_id=col_id(hop), device_id_type=MESH)

    pl.semaphore_wait(barrier, owners - 1 + count_cols - 1)

    right = (me + 1) % owners
    left = (me + owners - 1) % owners

    def block_copy(hop):
        target = (me + hop) % owners
        return pltpu.make_async_remote_copy(
            src_ref=blocks_ref.at[pl.ds(target * per_pair, per_pair)],
            dst_ref=recv.at[pl.ds(me * per_pair, per_pair)],
            send_sem=block_send.at[hop],
            recv_sem=block_recv.at[hop],
            device_id=owner_id(target),
            device_id_type=MESH,
        )

    def halo_copy(side):
        return pltpu.make_async_remote_copy(
            src_ref=panel_ref,
            dst_ref=ext_one.at[pl.ds(0 if side == 0 else 2 * br_dev, br_dev)],
            send_sem=halo_send.at[side],
            recv_sem=halo_recv.at[side],
            device_id=owner_id(right if side == 0 else left),
            device_id_type=MESH,
        )

    own_blocks = pltpu.make_async_copy(
        blocks_ref.at[pl.ds(me * per_pair, per_pair)],
        recv.at[pl.ds(me * per_pair, per_pair)],
        own_sem.at[0],
    )
    own_panel = pltpu.make_async_copy(panel_ref, ext_one.at[pl.ds(br_dev, br_dev)], own_sem.at[1])

    @pl.loop(1, owners)
    def _(step):
        half = owners // 2
        hop = (half + jnp.where(step % 2 == 0, step // 2, owners - step // 2)) % owners
        block_copy(hop).start()

    for side in (0, 1):
        halo_copy(side).start()
    own_blocks.start()
    own_panel.start()
    own_blocks.wait()
    own_panel.wait()
    for side in (0, 1):
        halo_copy(side).wait()

    @pl.loop(1, owners)
    def _(hop):
        block_copy(hop).wait()

    def row_copy(parts, send, receive, row, hop):
        return pltpu.make_async_remote_copy(
            src_ref=parts.at[my_col, row],
            dst_ref=parts.at[my_col, row],
            send_sem=send.at[row, hop],
            recv_sem=receive.at[row, hop],
            device_id=col_id(hop),
            device_id_type=MESH,
        )

    def multiply(ext, parts, send, receive):
        @pl.loop(0, br_dev)
        def _(row):
            base = row * kb_col
            lhs = jnp.concatenate([recv[order_ref[base + k]] for k in range(kb_col)], axis=1)
            rhs = jnp.concatenate([ext[cols_ref[base + k]] for k in range(kb_col)], axis=0)
            parts[my_col, row] = jnp.dot(lhs, rhs, preferred_element_type=jnp.float32)
            for hop in range(1, count_cols):
                row_copy(parts, send, receive, row, hop).start()

    def summed(parts, send, receive, row):
        for hop in range(1, count_cols):
            row_copy(parts, send, receive, row, hop).wait()
        total = parts[0, row]
        for col in range(1, count_cols):
            total = total + parts[col, row]
        return total

    def next_copy(row, side):
        return pltpu.make_async_remote_copy(
            src_ref=ext_two.at[br_dev + row],
            dst_ref=ext_two.at[row if side == 0 else 2 * br_dev + row],
            send_sem=next_send.at[row, side],
            recv_sem=next_recv.at[row, side],
            device_id=owner_id(right if side == 0 else left),
            device_id_type=MESH,
        )

    multiply(ext_one, parts_one, one_send, one_recv)

    @pl.loop(0, br_dev)
    def _(row):
        value = summed(parts_one, one_send, one_recv, row).astype(jnp.bfloat16)
        ext_two[br_dev + row] = value
        for side in (0, 1):
            next_copy(row, side).start()
        one_ref[row] = value

    @pl.loop(0, br_dev)
    def _(row):
        for side in (0, 1):
            next_copy(row, side).wait()

    multiply(ext_two, parts_two, two_send, two_recv)

    @pl.loop(0, br_dev)
    def _(row):
        total = summed(parts_two, two_send, two_recv, row)
        two_ref[row] = (2.0 * total - ext_one[br_dev + row].astype(jnp.float32)).astype(jnp.bfloat16)


def local(scf_blocks, scf_source, pattern, panel):
    br_dev, kb_col = pattern.shape
    slots, block_len, _ = scf_blocks.shape
    width = panel.shape[1]
    count_cols = lax.axis_size("cols")
    owners = lax.axis_size("rows") * lax.axis_size("sub")
    tiles = br_dev * owners
    me = lax.axis_index("rows") * lax.axis_size("sub") + lax.axis_index("sub")
    local_cols = ((pattern - (me - 1) * br_dev + tiles) % tiles).reshape(-1)
    order = scf_source.reshape(-1)
    tile = (block_len, width)
    out = jax.ShapeDtypeStruct((br_dev, *tile), jnp.bfloat16)
    vmem = pl.BlockSpec(memory_space=pltpu.VMEM)
    smem = pl.BlockSpec(memory_space=pltpu.SMEM)
    hbm = pl.BlockSpec(memory_space=pl.ANY)
    dma = pltpu.SemaphoreType.DMA
    one, two = pl.pallas_call(
        kernel,
        out_shape=(out, out),
        in_specs=[hbm, hbm, smem, smem],
        out_specs=(vmem, vmem),
        scratch_shapes=[
            pltpu.VMEM((slots, block_len, block_len), jnp.bfloat16),
            pltpu.VMEM((3 * br_dev, *tile), jnp.bfloat16),
            pltpu.VMEM((3 * br_dev, *tile), jnp.bfloat16),
            pltpu.VMEM((count_cols, br_dev, *tile), jnp.float32),
            pltpu.VMEM((count_cols, br_dev, *tile), jnp.float32),
            dma((2,)),
            dma((owners,)),
            dma((owners,)),
            dma((2,)),
            dma((2,)),
            dma((br_dev, 2)),
            dma((br_dev, 2)),
            dma((br_dev, count_cols)),
            dma((br_dev, count_cols)),
            dma((br_dev, count_cols)),
            dma((br_dev, count_cols)),
        ],
        compiler_params=pltpu.CompilerParams(
            collective_id=0, has_side_effects=True, vmem_limit_bytes=32 * 2**20
        ),
    )(scf_blocks, panel.reshape(br_dev, *tile), order, local_cols)
    return one.reshape(panel.shape), two.reshape(panel.shape)


def solution(mesh):
    return jax.shard_map(
        local,
        mesh=mesh,
        in_specs=(
            P(("groups", "rows", "cols", "sub"), None, None),
            P(("groups", "rows", "sub"), "cols"),
            P(("groups", "rows", "sub"), "cols"),
            P(("groups", "rows", "sub"), None),
        ),
        out_specs=(P(("groups", "rows", "sub"), None), P(("groups", "rows", "sub"), None)),
        check_vma=False,
    )
```

time: 226 us -> 162 us (0.72); the launches traced: 223 us -> 162 us
  Pallas kernels: 0 us -> 155 us
  waiting for transfers between devices: 151 us -> 0 us
  blocking collectives: 17.8 us -> 0 us
  between operations: 14.1 us -> 0.66 us
  starting transfers between devices: 10.3 us -> 0 us
  other arithmetic: 9.78 us -> 0.7 us
  matrix products: 7.1 us -> 0 us
  local copies, waits for them, and re-layouts: 12.4 us -> 5.82 us
    pallas_call x0 -> x1, Pallas kernels: none -> 155 us  [local(): pl.pallas_call(kernel, out_shape=(out, out), in_specs=[hbm, hbm, smem, sm...]
    ppermute x4 -> x0, waiting for transfers between devices: 113 us -> none  [the longest x2 113 us: padded(): lax.ppermute(head, axis, [((i + 1) % count, i) for i in range(count)])]
    psum x1 -> x0, waiting for transfers between devices: 38.7 us -> none  [combine_cols(): summed = lax.psum(partial_value, 'cols')]
    psum x1 -> x0, blocking collectives: 17.8 us -> none  [combine_cols(): summed = lax.psum(partial_value, 'cols')]
    gather x3 -> x0, local copies, waits for them, and re-layouts: 11.3 us -> none  [the longest x2 6.06 us: multiply(): jnp.take(tile_stack, local_cols, axis=0)]
    dot_general x2 -> x0, matrix products: 7.1 us -> none  [multiply(): jnp.einsum('bkij,bkjc->bic', blocks, picked, preferred_element_type=jnp.f...]
    select_n x5 -> x1, other arithmetic: 7.39 us -> 0.7 us  [local(): local_cols = ((pattern - (me - 1) * br_dev + tiles) % tiles).reshape(-1)]
    all_to_all x1 -> x0, starting transfers between devices: 5.78 us -> none  [local(): lax.all_to_all(scf_blocks, ('rows', 'sub'), split_axis=0, concat_axis=0,...]
  transfers between devices with their start and end apart: 6 -> 0, of which waited for: 3 -> 0; matrix products, arithmetic and copies ran while one was open for 4% -> 0% of each run, Pallas kernels for 0% -> 0%
where the time goes in v1:
time: 162 us
  Pallas kernels  155 us (96%)
  local copies, waits for them, and re-layouts  5.82 us (4%)
    pallas_call x1, Pallas kernels, local(): pl.pallas_call(kernel, out_shape=(out, out), in_specs=[hbm, hbm, smem, sm...  155 us
    unnamed x7, local copies, waits for them, and re-layouts  5.58 us

profile of v1, /device:TPU:11, one launch (start us, length us, event | category | flops | bytes accessed | tf_op | source)
XLA Modules:
  0.0 161.9 jit_solution(13700589861782609373)
XLA Ops:
  0.6 0.7 add_select_fusion
  1.3 0.1 copy.9
  1.4 0.1 reshape.21.cols_ref
  1.5 0.8 copy.8
  2.3 0.1 reshape.20.order_ref
  2.3 0.0 copy-start
  2.4 2.2 %copy-done = bf16[128,128,128]{2,1,0:T(8,128)(2,1)S(1)} copy-done((bf16[128,128,128]{2,1,0:T(8,128)(2,1)S(1)}, bf16[128,128,128]{2,1,0:T(8,128)(2,1)}, u32[]{:S(2)}) %copy-start) | copy-done | bytes 4194328
  4.5 0.0 copy-start.1
  4.5 1.0 copy-done.1
  5.6 154.7 %shard_map.59 = (bf16[16,128,128]{2,1,0:T(8,128)(2,1)S(1)}, bf16[16,128,128]{2,1,0:T(8,128)(2,1)S(1)}) custom-call(bf16[128,128,128]{2,1,0:T(8,128)(2,1)S(1)} %copy-done, bf16[16,128,128]{2,1,0:T(8,128)(2,1)S(1)} %bitcast.3, s32[128]{0:T(128)S(1)} %reshape.20.order_ref, s32[128]{0:T(128)S(1)} %reshape.21.cols_ref), custom_call_target="tpu_custom_call" | custom-call | tf_op jit(solution)/shard_map/pallas_call | solution.py:173
  160.3 0.8 copy.12
  161.1 0.8 copy.13
Async XLA Ops:
  2.3 2.2 %copy-start = (bf16[128,128,128]{2,1,0:T(8,128)(2,1)S(1)}, bf16[128,128,128]{2,1,0:T(8,128)(2,1)}, u32[]{:S(2)}) copy-start(bf16[128,128,128]{2,1,0:T(8,128)(2,1)} %blocks_ref.1) | copy-start | bytes 12582916
  4.5 1.0 copy-start.1

commit v2 on v1

v2 whole, which is shorter than its diff:
```python
import jax
import jax.numpy as jnp
from jax import lax
from jax.experimental import pallas as pl
from jax.experimental.pallas import tpu as pltpu
from jax.sharding import PartitionSpec as P

MESH = pl.DeviceIdType.MESH
SEND = jnp.bfloat16
VMEM_MIB = 32


def kernel(
    blocks_ref, panel_ref, order_ref, pattern_ref, one_ref, two_ref,
    recv, ext_one, ext_two, outbox, inbox, own, final,
    own_sem, block_send, block_recv, halo_send, halo_recv, pass_send, pass_recv,
    next_send, next_recv, sum_send, sum_recv, share_send, share_recv,
):
    slots = blocks_ref.shape[0]
    br_dev, kb_col = pattern_ref.shape
    count_sub = lax.axis_size("sub")
    count_cols = lax.axis_size("cols")
    owners = lax.axis_size("rows") * count_sub
    per_pair = slots // owners
    chunk = br_dev // count_cols
    tiles = owners * br_dev
    me = lax.axis_index("rows") * count_sub + lax.axis_index("sub")
    my_col = lax.axis_index("cols")
    right = (me + 1) % owners
    left = (me + owners - 1) % owners
    col_hops = range(1, count_cols)
    bases = (0, 2 * br_dev)

    def owner_id(owner):
        return {"rows": owner // count_sub, "sub": owner % count_sub}

    def col_id(hop):
        return {"cols": (my_col + hop) % count_cols}

    def remote(src, dst, send_sem, recv_sem, device_id):
        return pltpu.make_async_remote_copy(
            src_ref=src, dst_ref=dst, send_sem=send_sem, recv_sem=recv_sem,
            device_id=device_id, device_id_type=MESH,
        )

    barrier = pltpu.get_barrier_semaphore()

    @pl.loop(1, owners)
    def _(hop):
        pl.semaphore_signal(barrier, inc=1, device_id=owner_id((me + hop) % owners), device_id_type=MESH)

    for hop in col_hops:
        pl.semaphore_signal(barrier, inc=1, device_id=col_id(hop), device_id_type=MESH)
    pl.semaphore_wait(barrier, owners - 1 + count_cols - 1)

    def block_copy(target, slot):
        return remote(
            blocks_ref.at[pl.ds(target * per_pair, per_pair)],
            recv.at[pl.ds(me * per_pair, per_pair)],
            block_send.at[slot], block_recv.at[slot], owner_id(target),
        )

    def halo_copy(side):
        return remote(
            panel_ref.at[pl.ds(my_col * chunk, chunk)],
            ext_one.at[pl.ds(bases[side] + my_col * chunk, chunk)],
            halo_send.at[side], halo_recv.at[side], owner_id((right, left)[side]),
        )

    def pass_copy(side, hop):
        part = ext_one.at[pl.ds(bases[side] + my_col * chunk, chunk)]
        return remote(part, part, pass_send.at[side, hop], pass_recv.at[side, hop], col_id(hop))

    own_blocks = pltpu.make_async_copy(
        blocks_ref.at[pl.ds(me * per_pair, per_pair)],
        recv.at[pl.ds(me * per_pair, per_pair)],
        own_sem.at[0],
    )
    own_panel = pltpu.make_async_copy(panel_ref, ext_one.at[pl.ds(br_dev, br_dev)], own_sem.at[1])

    for side in (0, 1):
        halo_copy(side).start()

    if owners & (owners - 1):
        @pl.loop(1, owners)
        def _(hop):
            block_copy((me + hop) % owners, hop).start()
    else:
        half = owners // 2
        while half:
            base = me // (2 * half) * (2 * half)
            sibling = base + (1 - (me - base) // half) * half

            @pl.loop(0, half)
            def _(step, half=half, sibling=sibling):
                block_copy(sibling + (me + step) % half, half + step).start()

            half //= 2

    own_blocks.start()
    own_panel.start()
    for side in (0, 1):
        halo_copy(side).wait()
        for hop in col_hops:
            pass_copy(side, hop).start()
    own_blocks.wait()
    own_panel.wait()
    for side in (0, 1):
        for hop in col_hops:
            pass_copy(side, hop).wait()

    @pl.loop(1, owners)
    def _(slot):
        block_copy((me + slot) % owners, slot).wait()

    first_tile = (me - 1) * br_dev

    def product(ext, row):
        lhs, rhs = [], []
        for k in range(kb_col):
            tile = pattern_ref[row, k] - first_tile
            tile = jnp.where(tile < 0, tile + tiles, tile)
            tile = jnp.where(tile >= tiles, tile - tiles, tile)
            tile = jnp.minimum(tile, 3 * br_dev - 1)
            lhs.append(recv[order_ref[row, k]])
            rhs.append(ext[tile])
        return jnp.dot(
            jnp.concatenate(lhs, axis=1), jnp.concatenate(rhs, axis=0),
            preferred_element_type=jnp.float32,
        )

    def sum_copy(turn, hop, step):
        row = (my_col + hop) % count_cols * chunk + step
        return remote(
            outbox.at[turn, row], inbox.at[turn, hop, step],
            sum_send.at[turn, hop, step], sum_recv.at[turn, hop, step], col_id(hop),
        )

    def multiply(ext, turn):
        for hop in col_hops:
            @pl.loop(0, chunk)
            def _(step, hop=hop):
                row = (my_col + hop) % count_cols * chunk + step
                outbox[turn, row] = product(ext, row).astype(SEND)
                sum_copy(turn, hop, step).start()

        @pl.loop(0, chunk)
        def _(step):
            own[step] = product(ext, my_col * chunk + step)

    def summed(turn, step):
        total = own[step]
        for hop in col_hops:
            sum_copy(turn, hop, step).wait()
            total = total + inbox[turn, hop, step].astype(jnp.float32)
        return total

    def share_copy(turn, ref, base, hop, step):
        part = ref.at[base + my_col * chunk + step]
        return remote(
            part, part, share_send.at[turn, hop, step], share_recv.at[turn, hop, step], col_id(hop)
        )

    def next_copy(row, side):
        return remote(
            ext_two.at[br_dev + row], ext_two.at[bases[side] + row],
            next_send.at[row, side], next_recv.at[row, side], owner_id((right, left)[side]),
        )

    multiply(ext_one, 0)

    @pl.loop(0, chunk)
    def _(step):
        row = my_col * chunk + step
        ext_two[br_dev + row] = summed(0, step).astype(jnp.bfloat16)
        for hop in col_hops:
            share_copy(0, ext_two, br_dev, hop, step).start()
        for side in (0, 1):
            next_copy(row, side).start()

    for hop in col_hops:
        @pl.loop(0, chunk)
        def _(step, hop=hop):
            share_copy(0, ext_two, br_dev, hop, step).wait()
            row = (my_col + count_cols - hop) % count_cols * chunk + step
            for side in (0, 1):
                next_copy(row, side).start()

    out_one = pltpu.make_async_copy(ext_two.at[pl.ds(br_dev, br_dev)], one_ref, own_sem.at[2])
    out_one.start()

    @pl.loop(0, br_dev)
    def _(row):
        for side in (0, 1):
            next_copy(row, side).wait()

    multiply(ext_two, 1)

    @pl.loop(0, chunk)
    def _(step):
        row = my_col * chunk + step
        total = 2.0 * summed(1, step) - ext_one[br_dev + row].astype(jnp.float32)
        final[row] = total.astype(jnp.bfloat16)
        for hop in col_hops:
            share_copy(1, final, 0, hop, step).start()

    for hop in col_hops:
        @pl.loop(0, chunk)
        def _(step, hop=hop):
            share_copy(1, final, 0, hop, step).wait()

    out_two = pltpu.make_async_copy(final, two_ref, own_sem.at[3])
    out_two.start()
    out_one.wait()
    out_two.wait()


def local(scf_blocks, scf_source, pattern, panel):
    br_dev, kb_col = pattern.shape
    slots, block_len, _ = scf_blocks.shape
    tile = (block_len, panel.shape[1])
    count_cols = lax.axis_size("cols")
    owners = lax.axis_size("rows") * lax.axis_size("sub")
    chunk = br_dev // count_cols
    out = jax.ShapeDtypeStruct((br_dev, *tile), jnp.bfloat16)
    smem = pl.BlockSpec(memory_space=pltpu.SMEM)
    hbm = pl.BlockSpec(memory_space=pl.ANY)
    dma = pltpu.SemaphoreType.DMA
    one, two = pl.pallas_call(
        kernel,
        out_shape=(out, out),
        in_specs=[hbm, hbm, smem, smem],
        out_specs=(hbm, hbm),
        scratch_shapes=[
            pltpu.VMEM((slots, block_len, block_len), jnp.bfloat16),
            pltpu.VMEM((3 * br_dev, *tile), jnp.bfloat16),
            pltpu.VMEM((3 * br_dev, *tile), jnp.bfloat16),
            pltpu.VMEM((2, br_dev, *tile), SEND),
            pltpu.VMEM((2, count_cols, chunk, *tile), SEND),
            pltpu.VMEM((chunk, *tile), jnp.float32),
            pltpu.VMEM((br_dev, *tile), jnp.bfloat16),
            dma((4,)),
            dma((owners,)),
            dma((owners,)),
            dma((2,)),
            dma((2,)),
            dma((2, count_cols)),
            dma((2, count_cols)),
            dma((br_dev, 2)),
            dma((br_dev, 2)),
            dma((2, count_cols, chunk)),
            dma((2, count_cols, chunk)),
            dma((2, count_cols, chunk)),
            dma((2, count_cols, chunk)),
        ],
        compiler_params=pltpu.CompilerParams(
            collective_id=0, has_side_effects=True, vmem_limit_bytes=VMEM_MIB * 2**20
        ),
    )(scf_blocks, panel.reshape(br_dev, *tile), scf_source, pattern)
    return one.reshape(panel.shape), two.reshape(panel.shape)


def solution(mesh):
    return jax.shard_map(
        local,
        mesh=mesh,
        in_specs=(
            P(("groups", "rows", "cols", "sub"), None, None),
            P(("groups", "rows", "sub"), "cols"),
            P(("groups", "rows", "sub"), "cols"),
            P(("groups", "rows", "sub"), None),
        ),
        out_specs=(P(("groups", "rows", "sub"), None), P(("groups", "rows", "sub"), None)),
        check_vma=False,
    )
```

time: 162 us -> 141 us (0.87); the launches traced: 162 us -> 139 us
  Pallas kernels: 155 us -> 132 us
    pallas_call x1, Pallas kernels: 155 us -> 132 us  [local(): pl.pallas_call(kernel, out_shape=(out, out), in_specs=[hbm, hbm, smem, sm...]
    unnamed x7 -> x8, local copies, waits for them, and re-layouts: 5.58 us -> 6.33 us
where the time goes in v2:
time: 141 us; the launch traced here: 139 us
  Pallas kernels  132 us (94%)
  local copies, waits for them, and re-layouts  6.33 us (4%)
    pallas_call x1, Pallas kernels, local(): pl.pallas_call(kernel, out_shape=(out, out), in_specs=[hbm, hbm, smem, sm...  132 us
    unnamed x8, local copies, waits for them, and re-layouts  6.33 us

profile of v2, /device:TPU:11, one launch (start us, length us, event | category | flops | bytes accessed | tf_op | source)
XLA Modules:
  0.0 138.8 jit_solution(3645041180628413969)
XLA Ops:
  0.6 0.8 copy.6.order_ref
  1.4 0.8 copy.7.pattern_ref
  2.1 0.0 copy-start
  2.1 2.2 %copy-done = bf16[128,128,128]{2,1,0:T(8,128)(2,1)S(1)} copy-done((bf16[128,128,128]{2,1,0:T(8,128)(2,1)S(1)}, bf16[128,128,128]{2,1,0:T(8,128)(2,1)}, u32[]{:S(2)}) %copy-start) | copy-done | bytes 4194328
  4.3 0.0 copy-start.1
  4.3 1.0 copy-done.1
  5.4 131.9 %shard_map.59 = (bf16[16,128,128]{2,1,0:T(8,128)(2,1)S(1)}, bf16[16,128,128]{2,1,0:T(8,128)(2,1)S(1)}) custom-call(bf16[128,128,128]{2,1,0:T(8,128)(2,1)S(1)} %copy-done, bf16[16,128,128]{2,1,0:T(8,128)(2,1)S(1)} %bitcast.3, s32[16,8]{1,0:T(8,128)S(1)} %copy.6.order_ref, s32[16,8]{1,0:T(8,128)S(1)} %copy.7.pattern_ref), custom_call_target="tpu_custom_call" | custom-call | tf_op jit(solution)/shard_map/pallas_call | solution.py:229
  137.3 0.8 copy.10
  138.0 0.8 copy.11
Async XLA Ops:
  2.1 2.2 %copy-start = (bf16[128,128,128]{2,1,0:T(8,128)(2,1)S(1)}, bf16[128,128,128]{2,1,0:T(8,128)(2,1)}, u32[]{:S(2)}) copy-start(bf16[128,128,128]{2,1,0:T(8,128)(2,1)} %blocks_ref.1) | copy-start | bytes 12582916
  4.3 1.0 copy-start.1

commit v3 on v2

--- a/solution.py
+++ b/solution.py
@@ -45,20 +45,64 @@
 
     barrier = pltpu.get_barrier_semaphore()
 
-    @pl.loop(1, owners)
-    def _(hop):
-        pl.semaphore_signal(barrier, inc=1, device_id=owner_id((me + hop) % owners), device_id_type=MESH)
-
-    for hop in col_hops:
-        pl.semaphore_signal(barrier, inc=1, device_id=col_id(hop), device_id_type=MESH)
-    pl.semaphore_wait(barrier, owners - 1 + count_cols - 1)
-
     def block_copy(target, slot):
         return remote(
             blocks_ref.at[pl.ds(target * per_pair, per_pair)],
             recv.at[pl.ds(me * per_pair, per_pair)],
             block_send.at[slot], block_recv.at[slot], owner_id(target),
         )
+
+    middle = lax.axis_size("rows") // 2
+    early = 2 * count_sub
+    late = owners - early
+    first_early = (middle - 1) * count_sub
+    first_late = first_early + early
+    my_row = lax.axis_index("rows")
+    is_early = (my_row == middle) | (my_row == middle - 1)
+    facing = 2 * middle - 1 - my_row
+
+    def greet(owner):
+        pl.semaphore_signal(barrier, inc=1, device_id=owner_id(owner), device_id_type=MESH)
+
+    def greet_cols():
+        for hop in col_hops:
+            pl.semaphore_signal(barrier, inc=1, device_id=col_id(hop), device_id_type=MESH)
+
+    @pl.when(is_early)
+    def _():
+        @pl.loop(1, early)
+        def _(hop):
+            greet(first_early + (me - first_early + hop) % early)
+
+        greet_cols()
+        pl.semaphore_wait(barrier, early - 1 + count_cols - 1)
+
+        @pl.loop(0, count_sub)
+        def _(step):
+            half = owners // 2
+            target = facing * count_sub + step
+            block_copy(target, half + (target - me + owners) % half).start()
+
+        @pl.loop(0, late)
+        def _(step):
+            greet((first_late + step) % owners)
+
+        pl.semaphore_wait(barrier, late)
+
+    @pl.when(jnp.logical_not(is_early))
+    def _():
+        place = (me + owners - first_late) % owners
+
+        @pl.loop(1, late)
+        def _(hop):
+            greet((first_late + (place + hop) % late) % owners)
+
+        greet_cols()
+        pl.semaphore_wait(barrier, owners - 1 + count_cols - 1)
+
+        @pl.loop(0, early)
+        def _(step):
+            greet(first_early + step)
 
     def halo_copy(side):
         return remote(
@@ -81,21 +125,22 @@
     for side in (0, 1):
         halo_copy(side).start()
 
-    if owners & (owners - 1):
-        @pl.loop(1, owners)
-        def _(hop):
-            block_copy((me + hop) % owners, hop).start()
-    else:
-        half = owners // 2
-        while half:
-            base = me // (2 * half) * (2 * half)
-            sibling = base + (1 - (me - base) // half) * half
-
-            @pl.loop(0, half)
-            def _(step, half=half, sibling=sibling):
-                block_copy(sibling + (me + step) % half, half + step).start()
-
-            half //= 2
+    half = owners // 2
+    while half:
+        base = me // (2 * half) * (2 * half)
+        sibling = base + (1 - (me - base) // half) * half
+
+        @pl.loop(0, half)
+        def _(step, half=half, sibling=sibling):
+            target = sibling + (me + step) % half
+            if half == owners // 2:
+                @pl.when(jnp.logical_not(is_early & (target // count_sub == facing)))
+                def _():
+                    block_copy(target, half + step).start()
+            else:
+                block_copy(target, half + step).start()
+
+        half //= 2
 
     own_blocks.start()
     own_panel.start()
@@ -138,13 +183,13 @@
 
     def multiply(ext, turn):
         for hop in col_hops:
-            @pl.loop(0, chunk)
+            @pl.loop(0, chunk, unroll=chunk)
             def _(step, hop=hop):
                 row = (my_col + hop) % count_cols * chunk + step
                 outbox[turn, row] = product(ext, row).astype(SEND)
                 sum_copy(turn, hop, step).start()
 
-        @pl.loop(0, chunk)
+        @pl.loop(0, chunk, unroll=chunk)
         def _(step):
             own[step] = product(ext, my_col * chunk + step)
 

time: 141 us -> 137 us (0.972); the launches traced: 139 us -> 137 us
  Pallas kernels: 132 us -> 130 us
    pallas_call x1, Pallas kernels: 132 us -> 130 us  [local(): pl.pallas_call(kernel, out_shape=(out, out), in_specs=[hbm, hbm, smem, sm...]
where the time goes in v3:
time: 137 us
  Pallas kernels  130 us (95%)
  local copies, waits for them, and re-layouts  6.33 us (5%)
    pallas_call x1, Pallas kernels, local(): pl.pallas_call(kernel, out_shape=(out, out), in_specs=[hbm, hbm, smem, sm...  130 us
    unnamed x8, local copies, waits for them, and re-layouts  6.33 us

profile of v3, /device:TPU:11, one launch (start us, length us, event | category | flops | bytes accessed | tf_op | source)
XLA Modules:
  0.0 136.6 jit_solution(9323984157639196300)
XLA Ops:
  0.6 0.8 copy.6.order_ref
  1.4 0.8 copy.7.pattern_ref
  2.1 0.0 copy-start
  2.1 2.2 %copy-done = bf16[128,128,128]{2,1,0:T(8,128)(2,1)S(1)} copy-done((bf16[128,128,128]{2,1,0:T(8,128)(2,1)S(1)}, bf16[128,128,128]{2,1,0:T(8,128)(2,1)}, u32[]{:S(2)}) %copy-start) | copy-done | bytes 4194328
  4.3 0.0 copy-start.1
  4.3 1.0 copy-done.1
  5.4 129.7 %shard_map.59 = (bf16[16,128,128]{2,1,0:T(8,128)(2,1)S(1)}, bf16[16,128,128]{2,1,0:T(8,128)(2,1)S(1)}) custom-call(bf16[128,128,128]{2,1,0:T(8,128)(2,1)S(1)} %copy-done, bf16[16,128,128]{2,1,0:T(8,128)(2,1)S(1)} %bitcast.3, s32[16,8]{1,0:T(8,128)S(1)} %copy.6.order_ref, s32[16,8]{1,0:T(8,128)S(1)} %copy.7.pattern_ref), custom_call_target="tpu_custom_call" | custom-call | tf_op jit(solution)/shard_map/pallas_call | solution.py:274
  135.0 0.8 copy.10
  135.8 0.8 copy.11
Async XLA Ops:
  2.1 2.2 %copy-start = (bf16[128,128,128]{2,1,0:T(8,128)(2,1)S(1)}, bf16[128,128,128]{2,1,0:T(8,128)(2,1)}, u32[]{:S(2)}) copy-start(bf16[128,128,128]{2,1,0:T(8,128)(2,1)} %blocks_ref.1) | copy-start | bytes 12582916
  4.3 1.0 copy-start.1

commit v4 on v3

--- a/solution.py
+++ b/solution.py
@@ -7,7 +7,7 @@
 
 MESH = pl.DeviceIdType.MESH
 SEND = jnp.bfloat16
-VMEM_MIB = 32
+VMEM_MIB = 57
 
 
 def kernel(
@@ -17,7 +17,7 @@
     next_send, next_recv, sum_send, sum_recv, share_send, share_recv,
 ):
     slots = blocks_ref.shape[0]
-    br_dev, kb_col = pattern_ref.shape
+    kb_col, br_dev = pattern_ref.shape
     count_sub = lax.axis_size("sub")
     count_cols = lax.axis_size("cols")
     owners = lax.axis_size("rows") * count_sub
@@ -163,11 +163,11 @@
     def product(ext, row):
         lhs, rhs = [], []
         for k in range(kb_col):
-            tile = pattern_ref[row, k] - first_tile
+            tile = pattern_ref[k, row] - first_tile
             tile = jnp.where(tile < 0, tile + tiles, tile)
             tile = jnp.where(tile >= tiles, tile - tiles, tile)
             tile = jnp.minimum(tile, 3 * br_dev - 1)
-            lhs.append(recv[order_ref[row, k]])
+            lhs.append(recv[order_ref[k, row]])
             rhs.append(ext[tile])
         return jnp.dot(
             jnp.concatenate(lhs, axis=1), jnp.concatenate(rhs, axis=0),
@@ -301,7 +301,7 @@
         compiler_params=pltpu.CompilerParams(
             collective_id=0, has_side_effects=True, vmem_limit_bytes=VMEM_MIB * 2**20
         ),
-    )(scf_blocks, panel.reshape(br_dev, *tile), scf_source, pattern)
+    )(scf_blocks, panel.reshape(br_dev, *tile), scf_source.T, pattern.T)
     return one.reshape(panel.shape), two.reshape(panel.shape)
 
 

time: 137 us -> 135 us (0.985)
  local copies, waits for them, and re-layouts: 6.33 us -> 3.74 us
    unnamed x8 -> x2, local copies, waits for them, and re-layouts: 6.33 us -> 3.74 us
where the time goes in v4:
time: 135 us
  Pallas kernels  131 us (97%)
  local copies, waits for them, and re-layouts  3.74 us (3%)
    pallas_call x1, Pallas kernels, local(): pl.pallas_call(kernel, out_shape=(out, out), in_specs=[hbm, hbm, smem, sm...  131 us
    unnamed x2, local copies, waits for them, and re-layouts  3.74 us

profile of v4, /device:TPU:11, one launch (start us, length us, event | category | flops | bytes accessed | tf_op | source)
XLA Modules:
  0.0 135.1 jit_solution(3495340268680245157)
XLA Ops:
  0.6 130.7 %shard_map.59 = (bf16[16,128,128]{2,1,0:T(8,128)(2,1)}, bf16[16,128,128]{2,1,0:T(8,128)(2,1)}) custom-call(bf16[128,128,128]{2,1,0:T(8,128)(2,1)} %blocks_ref.1, bf16[16,128,128]{2,1,0:T(8,128)(2,1)} %bitcast.5, s32[8,16]{1,0:T(8,128)} %bitcast.8, s32[8,16]{1,0:T(8,128)} %bitcast.9), custom_call_target="tpu_custom_call" | custom-call | tf_op jit(solution)/shard_map/pallas_call | solution.py:274
  131.3 1.9 %copy.8 = bf16[2048,128]{1,0:T(8,128)(2,1)} copy(bf16[2048,128]{1,0:T(8,128)(2,1)} %bitcast.7) | data formatting | bytes 1048576
  133.2 1.9 %copy.9 = bf16[2048,128]{1,0:T(8,128)(2,1)} copy(bf16[2048,128]{1,0:T(8,128)(2,1)} %bitcast.6) | data formatting | bytes 1048576
